TPU v7x, 32 devices: a whole 2x2x4 slice. The times are simulated.
32 devices in a mesh: groups: 2 (over x), rows: 8 (over z, y), sub: 2 (over core).
Axes of the slice: x: 2, y: 2, z: 4, core: 2. Of those that a mesh axis runs over, the one named last changes fastest.
Arguments:
- database: bfloat16 [49152, 1536], P(('groups', 'rows', 'sub')), parts along dimension 0, may hold values from -6 to 6
- queries: bfloat16 [256, 1536], P(('groups', 'rows', 'sub')), parts along dimension 0, may hold values from -0.15625 to 0.15625
- probes: int32 [256, 12], P('groups'), parts along dimension 0, may hold values from 0 to 47, all different within a row
- block_list: int32 [384, 1], P(('groups', 'rows', 'sub')), parts along dimension 0, may hold values from 0 to 47
- neighbors: int32 [384, 8], P(('groups', 'rows', 'sub')), parts along dimension 0, may hold values from 0 to 191, as said below
- affinity: float32 [384, 8, 128, 128], P(('groups', 'rows', 'sub')), parts along dimension 0, may hold values from 0 to 10, as said below
Outputs:
- diffused: float32 [49152, 128], P(('groups', 'rows', 'sub')), parts along dimension 0
There are 2 independent parts, one for each index of `groups`. A program takes and returns all parts, laid end to end along the dimension named above; each array names one. Nothing has to cross between parts.
Inputs may be any that keep to these rules, and one draw needn't show every extreme that they name: Column 0 names the block itself. For every other column j the blocks are paired two by two: neighbors[b, j] = c exactly when neighbors[c, j] = b, with c != b, and c lies among the blocks of the same device or among the nearer 12 // 2 blocks of an adjacent device along the row blocks. Entries are positive. The matrix W is symmetric: affinity[neighbors[b, j], j] is the transpose of affinity[b, j], and affinity[b, 0] is symmetric.
All inputs are finite; a program needn't handle non-finite values.
Results may differ from a plain program's by a relative error of at most 0.0003.
Values may be sent and summed in bfloat16 or wider, within the bound.
A program may use at most 64 MiB of HBM per device.

v0:
```python
import jax
import jax.numpy as jnp
from jax import lax
from jax.sharding import PartitionSpec as P

ITERS = 3


damping = 0.99


def with_halo(shard, sides, width):
    for axis, dim in sides:
        count, length = (lax.axis_size(axis), shard.shape[dim])
        up = [(i, (i + 1) % count) for i in range(count - 1)]
        down = [(j, i) for i, j in up]
        last = lax.slice_in_dim(shard, length - width, length, axis=dim)
        initial = lax.slice_in_dim(shard, 0, width, axis=dim)
        before = lax.ppermute(last, axis, up)
        after = lax.ppermute(initial, axis, down)
        shard = jnp.concatenate([before, shard, after], axis=dim)
    return shard


def squares(residual):
    return lax.psum(jnp.sum(residual * residual, axis=0), ("rows", "sub"))


def on_device(database, queries, probes, block_list, neighbors, affinity):
    block_count = affinity.shape[0]
    block_rows = affinity.shape[2]
    query_count = probes.shape[0]
    half_blocks = block_count // 2
    scores = lax.dot_general(
        database,
        lax.all_gather(queries, ("rows", "sub"), axis=0, tiled=True),
        (((1,), (1,)), ((), ())),
        preferred_element_type=jnp.float32,
    )
    probed = jnp.any(block_list[:, 0][:, None, None] == probes[None, :, :], axis=2)
    grown = jnp.exp(scores).reshape(block_count, block_rows, query_count)
    seed_rows = jnp.where(probed[:, None, :], grown, jnp.zeros_like(grown)).reshape(-1, query_count)
    degree = jnp.sum(affinity, axis=(1, 3)).reshape(-1, 1)
    inv_root = 1.0 / jnp.sqrt(degree)
    position = lax.axis_index(("rows", "sub"))
    local_slot = neighbors - position * block_count + half_blocks
    diffused = jnp.zeros_like(seed_rows)
    residual = seed_rows
    direction = seed_rows
    norm_now = squares(residual)
    for turn_index in range(ITERS):
        scaled = inv_root * direction
        widened = with_halo(scaled, ((("rows", "sub"), 0),), scaled.shape[0] // 2)
        stacked = widened.reshape(2 * block_count, block_rows, query_count)
        picked = stacked[local_slot]
        product = jnp.einsum("ijrs,ijsq->irq", affinity, picked, precision=lax.Precision.HIGHEST)
        image = direction - damping * inv_root * product.reshape(direction.shape)
        step_size = norm_now / lax.psum(jnp.sum(direction * image, axis=0), ("rows", "sub"))
        diffused = diffused + step_size * direction
        residual = residual - step_size * image
        norm_next = squares(residual)
        direction = residual + norm_next / norm_now * direction
        norm_now = norm_next
    return diffused


def solution(mesh):
    placed = (
        P(("groups", "rows", "sub"), None),
        P(("groups", "rows", "sub"), None),
        P("groups", None),
        P(("groups", "rows", "sub"), None),
        P(("groups", "rows", "sub"), None),
        P(("groups", "rows", "sub"), None, None, None),
    )
    return jax.shard_map(
        on_device,
        mesh=mesh,
        in_specs=placed,
        out_specs=P(("groups", "rows", "sub"), None),
        check_vma=False,
    )
```

profile of v0, /device:TPU:0, one launch (start us, length us, event | category | flops | bytes accessed | tf_op | source)
XLA Modules:
  0.0 259.3 jit_solution(14299471537103719863)
XLA Ops:
  0.0 0.0 copy-start.7
  0.0 0.0 copy-start.10
  0.0 0.0 copy-start.8
  0.0 3.2 %reduce_sum.64 = f32[12,128]{1,0:T(8,128)S(1)} reduce(f32[12,8,128,128]{3,2,1,0:T(8,128)} %param.11, f32[]{:T(128)} %constant.11.clone.1), dimensions={1,3}, to_apply=%region_3.4 | reduce | flops 1571328 | bytes 6297604 | tf_op jit(solution)/shard_map/reduce_sum | solution.py:43
  3.2 0.0 copy-start.9
  3.2 0.0 copy-done.7
  3.2 0.0 copy-start.5
  3.2 24.2 %all_gather.3 = bf16[128,1536]{1,0:T(8,128)(2,1)S(1)} all-gather(bf16[8,1536]{1,0:T(8,128)(2,1)S(1)} %copy-done.7), channel_id=1, replica_groups=mesh['groups'=2,'rows'=8,'sub'=2] {'rows','sub'}, dimensions={0}, use_global_device_ids=true | all-gather | bytes 417792 | tf_op jit(solution)/shard_map/all_gather | solution.py:36
  27.4 0.0 copy-done.10
  27.4 0.0 copy-done.8
  27.4 0.1 compare_reduce_fusion
  27.5 0.1 broadcast_in_dim.14
  27.6 3.7 %broadcast_multiply_fusion.2 = (f32[1536,128]{1,0:T(8,128)S(1)}, f32[1536,128]{1,0:T(8,128)S(1)}) fusion(f32[1536]{0:T(1024)S(1)} %rsqrt_bitcast_fusion, pred[1536,128]{1,0:T(32,128)(4,1)S(1)} %bitcast.70, bf16[1536,1536]{1,0:T(8,128)(2,1)} %param.6, bf16[128,1536]{1,0:T(8,128)(2,1)S(1)} %all_gather.3), kind=kOutput, calls=%fused_computation.27 | convolution fusion | flops 604372992 | bytes 6887424 | tf_op jit(solution)/shard_map/dot_general | solution.py:34
  31.3 0.1 fusion.6
  31.4 2.3 collective-permute-start
  33.7 1.3 collective-permute-start.1
  35.0 0.0 copy-done.5
  35.0 0.0 copy-done.9
  35.0 0.1 copy.11
  35.1 0.1 reshape.51
  35.2 0.0 collective-permute-done
  35.2 2.2 collective-permute-done.1
  37.4 1.1 pad_maximum_fusion
  38.5 3.6 %gather_fusion = f32[96,128,128]{2,1,0:T(8,128)} fusion(f32[24,128,128]{2,1,0:T(8,128)S(1)} %bitcast.65, s32[1024]{0:T(1024)S(1)} %pad_clamp_fusion), kind=kCustom, calls=%fused_computation | custom fusion | bytes 12583296 | tf_op jit(solution)/shard_map/gather | solution.py:55
  42.1 0.0 copy-start.6
  42.1 9.6 %fusion.7 = f32[12,128,128,1]{1,2,3,0:T(8,128)S(1)} fusion(f32[12,8,128,128]{3,2,1,0:T(8,128)} %bitcast.68, f32[12,8,128,128]{3,2,1,0:T(8,128)} %param.11), kind=kOutput, calls=%fused_computation.36 | convolution fusion | flops 2415919104 | bytes 13369344 | tf_op jit(solution)/shard_map/ijrs,ijsq->irq/dot_general | solution.py:56
  51.8 0.0 copy-start
  51.8 0.3 multiply_reduce_fusion.3
  52.1 34.9 %all-reduce = (f32[128]{0:T(128)S(1)}, f32[128]{0:T(128)S(1)}) all-reduce(f32[128]{0:T(128)S(1)} %get-tuple-element.6, f32[128]{0:T(128)S(1)} %get-tuple-element.5), channel_id=1, replica_groups=mesh['groups'=2,'rows'=8,'sub'=2] {'rows','sub'}, use_global_device_ids=true, to_apply=%region_2.3 | all-reduce | flops 256 | bytes 2048 | tf_op jit(solution)/shard_map/psum | solution.py:26
  87.0 0.3 multiply_reduce_fusion.2
  87.3 29.5 %psum.44 = f32[128]{0:T(128)S(1)} all-reduce(f32[128]{0:T(128)S(1)} %multiply_reduce_fusion.2), channel_id=1, replica_groups=mesh['groups'=2,'rows'=8,'sub'=2] {'rows','sub'}, use_global_device_ids=true, to_apply=%region_7.8 | all-reduce | flops 128 | bytes 1024 | tf_op jit(solution)/shard_map/psum | solution.py:26
  116.8 0.0 copy-done.6
  116.8 0.5 broadcast_multiply_fusion.1
  117.3 0.1 fusion.5
  117.3 1.8 collective-permute-start.2
  119.1 1.5 collective-permute-start.3
  120.6 0.0 collective-permute-done.2
  120.6 0.0 copy-done
  120.6 2.1 collective-permute-done.3
  122.8 0.1 pad_maximum_fusion.1
  122.9 3.6 %gather_fusion.1 = f32[96,128,128]{2,1,0:T(8,128)} fusion(f32[24,128,128]{2,1,0:T(8,128)S(1)} %bitcast.66, s32[1024]{0:T(1024)S(1)} %pad_clamp_fusion), kind=kCustom, calls=%fused_computation.1 | custom fusion | bytes 12583296 | tf_op jit(solution)/shard_map/gather | solution.py:55
  126.5 9.9 %fusion.8 = f32[12,128,128,1]{1,2,3,0:T(8,128)S(1)} fusion(f32[12,8,128,128]{3,2,1,0:T(8,128)} %bitcast.69, f32[12,8,128,128]{3,2,1,0:T(8,128)} %param.11), kind=kOutput, calls=%fused_computation.37 | convolution fusion | flops 2415919104 | bytes 13369344 | tf_op jit(solution)/shard_map/ijrs,ijsq->irq/dot_general | solution.py:56
  136.4 0.0 copy-start.4
  136.4 0.9 copy-done.4
  137.3 0.3 multiply_reduce_fusion.1
  137.6 35.0 %psum.45 = f32[128]{0:T(128)S(1)} all-reduce(f32[128]{0:T(128)S(1)} %multiply_reduce_fusion.1), channel_id=1, replica_groups=mesh['groups'=2,'rows'=8,'sub'=2] {'rows','sub'}, use_global_device_ids=true, to_apply=%region_9.10 | all-reduce | flops 128 | bytes 1024 | tf_op jit(solution)/shard_map/psum | solution.py:58
  172.5 0.0 copy-done.1
  172.5 1.5 multiply_reduce_fusion
  174.0 0.0 copy-start.2
  174.0 29.5 %psum.46 = f32[128]{0:T(128)S(1)} all-reduce(f32[128]{0:T(128)S(1)} %get-tuple-element.9), channel_id=1, replica_groups=mesh['groups'=2,'rows'=8,'sub'=2] {'rows','sub'}, use_global_device_ids=true, to_apply=%region_11.12 | all-reduce | flops 128 | bytes 1024 | tf_op jit(solution)/shard_map/psum | solution.py:26
  203.5 0.3 broadcast_multiply_fusion
  203.8 0.1 fusion.4
  203.9 1.8 collective-permute-start.4
  205.7 1.3 collective-permute-start.5
  207.0 0.0 collective-permute-done.4
  207.0 0.0 copy-done.2
  207.0 2.3 collective-permute-done.5
  209.3 0.1 pad_maximum_fusion.2
  209.4 3.6 %gather_fusion.2 = f32[96,128,128]{2,1,0:T(8,128)} fusion(f32[24,128,128]{2,1,0:T(8,128)S(1)} %bitcast.64, s32[1024]{0:T(1024)S(1)} %pad_clamp_fusion), kind=kCustom, calls=%fused_computation.2 | custom fusion | bytes 12583296 | tf_op jit(solution)/shard_map/gather | solution.py:55
  213.0 9.9 %fusion.9 = f32[12,128,128,1]{1,2,3,0:T(8,128)S(1)} fusion(f32[12,8,128,128]{3,2,1,0:T(8,128)} %bitcast.67, f32[12,8,128,128]{3,2,1,0:T(8,128)} %param.11), kind=kOutput, calls=%fused_computation.38 | convolution fusion | flops 2415919104 | bytes 13369344 | tf_op jit(solution)/shard_map/ijrs,ijsq->irq/dot_general | solution.py:56
  222.9 0.0 copy-done.3
  222.9 0.3 fusion.1
  223.2 35.0 %psum.47 = f32[128]{0:T(128)S(1)} all-reduce(f32[128]{0:T(128)S(1)} %fusion.1), channel_id=1, replica_groups=mesh['groups'=2,'rows'=8,'sub'=2] {'rows','sub'}, use_global_device_ids=true, to_apply=%region_13.14 | all-reduce | flops 128 | bytes 1024 | tf_op jit(solution)/shard_map/psum | solution.py:58
  258.2 1.1 multiply_add_fusion
  (11 shorter events, 0.1 us)
Async XLA Ops:
  0.0 3.2 %copy-start.7 = (bf16[8,1536]{1,0:T(8,128)(2,1)S(1)}, bf16[8,1536]{1,0:T(8,128)(2,1)}, u32[]{:S(2)}) copy-start(bf16[8,1536]{1,0:T(8,128)(2,1)} %param.7) | copy-start | bytes 73732
  0.0 27.4 %copy-start.10 = (s32[12,1]{0,1:T(1,128)S(1)}, s32[12,1]{0,1:T(1,128)}, u32[]{:S(2)}) copy-start(s32[12,1]{0,1:T(1,128)} %param.9) | copy-start | bytes 148
  0.0 27.4 %copy-start.8 = (s32[128,12]{0,1:T(8,128)S(1)}, s32[128,12]{0,1:T(8,128)}, u32[]{:S(2)}) copy-start(s32[128,12]{0,1:T(8,128)} %param.8) | copy-start | bytes 18436
  3.2 31.8 %copy-start.9 = (s32[12,8]{0,1:T(8,128)S(1)}, s32[12,8]{0,1:T(8,128)}, u32[]{:S(2)}) copy-start(s32[12,8]{0,1:T(8,128)} %param.10) | copy-start | bytes 1156
  3.2 31.7 %copy-start.5 = (f32[1536]{0:T(1024)}, f32[1536]{0:T(1024)S(1)}, u32[]{:S(2)}) copy-start(f32[1536]{0:T(1024)S(1)} %rsqrt_bitcast_fusion) | copy-start | bytes 18436
  31.4 3.8 %collective-permute-start = (f32[768,128]{1,0:T(8,128)S(1)}, f32[768,128]{1,0:T(8,128)S(1)}, u32[]{:S(2)}, u32[]{:S(2)}) collective-permute-start(f32[768,128]{1,0:T(8,128)S(1)} %get-tuple-element.17), channel_id=1, source_target_pairs={{0,1},{1,2},{2,3},{3,4},{4,5},{5,6},{6,7},{7,8},{8,9},{9,10},{10,1... | collective-permute-start | bytes 1179656 | tf_op jit(solution)/shard_map/ppermute | solution.py:19
  33.7 3.7 %collective-permute-start.1 = (f32[768,128]{1,0:T(8,128)S(1)}, f32[768,128]{1,0:T(8,128)}, u32[]{:S(2)}, u32[]{:S(2)}) collective-permute-start(f32[768,128]{1,0:T(8,128)S(1)} %get-tuple-element.18), channel_id=1, source_target_pairs={{1,0},{2,1},{3,2},{4,3},{5,4},{6,5},{7,6},{8,7},{9,8},{10,9},{11,1... | collective-permute-start | bytes 1179656 | tf_op jit(solution)/shard_map/ppermute | solution.py:20
  42.1 74.7 %copy-start.6 = (f32[1536]{0:T(1024)S(1)}, f32[1536]{0:T(1024)}, u32[]{:S(2)}) copy-start(f32[1536]{0:T(1024)} %copy-done.5) | copy-start | bytes 18436
  51.8 68.9 %copy-start = (f32[12,128,128,1]{1,2,3,0:T(8,128)}, f32[12,128,128,1]{1,2,3,0:T(8,128)S(1)}, u32[]{:S(2)}) copy-start(f32[12,128,128,1]{1,2,3,0:T(8,128)S(1)} %fusion.7) | copy-start | bytes 2359300
  117.3 3.3 %collective-permute-start.2 = (f32[768,128]{1,0:T(8,128)S(1)}, f32[768,128]{1,0:T(8,128)S(1)}, u32[]{:S(2)}, u32[]{:S(2)}) collective-permute-start(f32[768,128]{1,0:T(8,128)S(1)} %get-tuple-element.15), channel_id=1, source_target_pairs={{0,1},{1,2},{2,3},{3,4},{4,5},{5,6},{6,7},{7,8},{8,9},{9,10},{10,1... | collective-permute-start | bytes 1179656 | tf_op jit(solution)/shard_map/ppermute | solution.py:19
  119.1 3.6 %collective-permute-start.3 = (f32[768,128]{1,0:T(8,128)S(1)}, f32[768,128]{1,0:T(8,128)S(1)}, u32[]{:S(2)}, u32[]{:S(2)}) collective-permute-start(f32[768,128]{1,0:T(8,128)S(1)} %get-tuple-element.16), channel_id=1, source_target_pairs={{1,0},{2,1},{3,2},{4,3},{5,4},{6,5},{7,6},{8,7},{9,8},{10,9},{11,1... | collective-permute-start | bytes 1179656 | tf_op jit(solution)/shard_map/ppermute | solution.py:20
  126.5 46.1 %copy-start.1 = (f32[12,128,128,1]{1,2,3,0:T(8,128)S(1)}, f32[12,128,128,1]{1,2,3,0:T(8,128)}, u32[]{:S(2)}) copy-start(f32[12,128,128,1]{1,2,3,0:T(8,128)} %copy-done) | copy-start | bytes 2359300
  136.4 0.9 copy-start.4
  174.0 33.0 %copy-start.2 = (f32[1536,128]{1,0:T(8,128)}, f32[1536,128]{1,0:T(8,128)S(1)}, u32[]{:S(2)}) copy-start(f32[1536,128]{1,0:T(8,128)S(1)} %get-tuple-element.10) | copy-start | bytes 2359300
  203.9 3.1 %collective-permute-start.4 = (f32[768,128]{1,0:T(8,128)S(1)}, f32[768,128]{1,0:T(8,128)S(1)}, u32[]{:S(2)}, u32[]{:S(2)}) collective-permute-start(f32[768,128]{1,0:T(8,128)S(1)} %get-tuple-element.13), channel_id=1, source_target_pairs={{0,1},{1,2},{2,3},{3,4},{4,5},{5,6},{6,7},{7,8},{8,9},{9,10},{10,1... | collective-permute-start | bytes 1179656 | tf_op jit(solution)/shard_map/ppermute | solution.py:19
  205.7 3.6 %collective-permute-start.5 = (f32[768,128]{1,0:T(8,128)S(1)}, f32[768,128]{1,0:T(8,128)S(1)}, u32[]{:S(2)}, u32[]{:S(2)}) collective-permute-start(f32[768,128]{1,0:T(8,128)S(1)} %get-tuple-element.14), channel_id=1, source_target_pairs={{1,0},{2,1},{3,2},{4,3},{5,4},{6,5},{7,6},{8,7},{9,8},{10,9},{11,1... | collective-permute-start | bytes 1179656 | tf_op jit(solution)/shard_map/ppermute | solution.py:20
  213.0 9.9 %copy-start.3 = (f32[1536,128]{1,0:T(8,128)S(1)}, f32[1536,128]{1,0:T(8,128)}, u32[]{:S(2)}) copy-start(f32[1536,128]{1,0:T(8,128)} %copy-done.2) | copy-start | bytes 2359300
where the time goes:
time: 260 us; the launch traced here: 259 us
  blocking collectives  188 us (72%)
  matrix products  33.1 us (13%)
  local copies, waits for them, and re-layouts  12.1 us (5%)
  starting transfers between devices  9.92 us (4%)
  other arithmetic  9.14 us (4%)
  waiting for transfers between devices  6.63 us (3%)
    psum x3, blocking collectives, squares(): return lax.psum(jnp.sum(residual * residual, axis=0), ('rows', 'sub'))  93.9 us
    psum x2, blocking collectives, on_device(): lax.psum(jnp.sum(direction * image, axis=0), ('rows', 'sub'))  69.9 us
    dot_general x3, matrix products, on_device(): jnp.einsum('ijrs,ijsq->irq', affinity, picked, precision=lax.Precision.HI...  29.4 us
    all_gather x1, blocking collectives, on_device(): lax.all_gather(queries, ('rows', 'sub'), axis=0, tiled=True)  24.2 us
    gather x3, local copies, waits for them, and re-layouts, on_device(): picked = stacked[local_slot]  10.8 us
    ppermute x3, waiting for transfers between devices, with_halo(): after = lax.ppermute(initial, axis, down)  6.62 us
    ppermute x3, starting transfers between devices, with_halo(): before = lax.ppermute(last, axis, up)  5.87 us
  transfers between devices with their start and end apart: 6, of which 3 were waited for; matrix products, arithmetic and copies ran while one was open for 0% of the time, Pallas kernels for 0%

commit v1 on v0

v1 whole, which is shorter than its diff:
```python
import functools

import jax
import jax.numpy as jnp
from jax import lax
from jax.experimental import pallas as pl
from jax.experimental.pallas import tpu as pltpu
from jax.sharding import PartitionSpec as P

ITERS = 3
damping = 0.99
PARTS = 2
MESH = pl.DeviceIdType.MESH
f32, bf16 = jnp.float32, jnp.bfloat16


def kernel(
    n, sub, pad, own, split,
    nb_ref, bl_ref, probes_ref, q_ref, db_hbm, aff_hbm,
    out_ref,
    gathered, query, db, aff, wcat, root,
    v0, v1, v2, v3, base, wide0, res1, wide1, dir1, res2,
    red0, red1, red2,
    aff_sem, db_sem, own_sem, q_send, q_recv, halo_send, halo_recv, red_send, red_recv,
):
    nblk, cols, blk, _ = aff.shape
    half = nblk // 2
    queries = out_ref.shape[1]
    me = lax.axis_index("rows") * sub + lax.axis_index("sub")

    def place(index):
        return {"rows": index // sub, "sub": lax.rem(index, sub)}

    def aff_copy(b):
        return pltpu.make_async_copy(aff_hbm.at[b], aff.at[b], aff_sem.at[b])

    chunks = db_sem.shape[0]
    chunk = db.shape[0] // chunks

    def db_copy(i):
        rows = pl.ds(i * chunk, chunk)
        return pltpu.make_async_copy(db_hbm.at[rows], db.at[rows], db_sem.at[i])

    own_copy = pltpu.make_async_copy(q_ref, gathered.at[me], own_sem)
    own_copy.start()
    for b in range(nblk):
        aff_copy(b).start()
    for i in range(chunks):
        db_copy(i).start()

    for v in (v0, v1, v2, v3):
        v[:, :half] = jnp.zeros((2, half, blk, queries), bf16)
        v[:, half + nblk:] = jnp.zeros((2, half, blk, queries), bf16)

    barrier = pltpu.get_barrier_semaphore()

    @pl.loop(1, n)
    def _(i):
        pl.semaphore_signal(barrier, inc=1, device_id=place(lax.rem(me + i, n)), device_id_type=MESH)

    pl.semaphore_wait(barrier, n - 1)

    def q_copy(peer):
        return pltpu.make_async_remote_copy(
            src_ref=q_ref, dst_ref=gathered.at[me], send_sem=q_send.at[peer], recv_sem=q_recv.at[me],
            device_id=place(peer), device_id_type=MESH,
        )

    def q_arrival(peer):
        return pltpu.make_async_remote_copy(
            src_ref=q_ref, dst_ref=gathered.at[peer], send_sem=q_send.at[peer], recv_sem=q_recv.at[peer],
            device_id=place(peer), device_id_type=MESH,
        )

    @pl.loop(1, n)
    def _(i):
        q_copy(lax.rem(me + i, n)).start()

    @pl.loop(0, nblk)
    def _(b):
        aff_copy(b).wait()
        total = jnp.zeros((blk, blk), f32)
        for j in range(cols):
            w = aff[b, j]
            total = total + w
            hi = w.astype(bf16)
            wcat[b, :blk, j * blk:(j + 1) * blk] = hi
            wcat[b, blk:, j * blk:(j + 1) * blk] = (w - hi.astype(f32)).astype(bf16)
        degree = jnp.sum(total, axis=1, keepdims=True)
        root[b] = jnp.broadcast_to(1.0 / jnp.sqrt(degree), (blk, queries))

    def put(v, index, u):
        hi = u.astype(bf16)
        v[0, index] = hi
        v[1, index] = (u - hi.astype(f32)).astype(bf16)

    def halo_copy(v, k, down):
        start, land = (half, half + nblk) if down else (nblk, 0)
        side = 2 * k + down
        peer = jnp.maximum(me - 1, 0) if down else jnp.minimum(me + 1, n - 1)
        return pltpu.make_async_remote_copy(
            src_ref=v.at[pl.ds(0, PARTS), pl.ds(start, half)],
            dst_ref=v.at[pl.ds(0, PARTS), pl.ds(land, half)],
            send_sem=halo_send.at[side], recv_sem=halo_recv.at[side],
            device_id=place(peer), device_id_type=MESH,
        )

    def halo_start(v, k, both=True):
        @pl.when(me > 0)
        def _():
            halo_copy(v, k, 1).start()
        if both:
            @pl.when(me < n - 1)
            def _():
                halo_copy(v, k, 0).start()

    def halo_wait(v, k, both=True):
        @pl.when(me < n - 1)
        def _():
            halo_copy(v, k, 1).wait_recv()
        if both:
            @pl.when(me > 0)
            def _():
                halo_copy(v, k, 0).wait_recv()

    def halo_sent(v, k, both=True):
        @pl.when(me > 0)
        def _():
            halo_copy(v, k, 1).wait_send()
        if both:
            @pl.when(me < n - 1)
            def _():
                halo_copy(v, k, 0).wait_send()

    def red_copy(red, k, peer, slot):
        return pltpu.make_async_remote_copy(
            src_ref=red.at[me], dst_ref=red.at[slot], send_sem=red_send.at[k, peer], recv_sem=red_recv.at[k, slot],
            device_id=place(peer), device_id_type=MESH,
        )

    def reduce_start(red, k, first, second):
        red[me] = jnp.concatenate([first, second], axis=0)

        @pl.loop(1, n)
        def _(i):
            peer = lax.rem(me + i, n)
            red_copy(red, k, peer, me).start()

    def reduce_wait(red, k):
        @pl.loop(1, n)
        def _(i):
            peer = lax.rem(me + i, n)
            red_copy(red, k, peer, peer).wait_recv()

        total = jnp.sum(red[...], axis=0)
        return (
            jnp.sum(total[:8], axis=0, keepdims=True),
            jnp.sum(total[8:], axis=0, keepdims=True),
        )

    def fold(values):
        return jnp.sum(values.reshape(blk // 8, 8, queries), axis=0)

    def weighed(v, b):
        picks = []
        for j in range(cols):
            slot = jnp.clip(nb_ref[b, j] - me * nblk + half, 0, 2 * nblk - 1)
            picks.append(jnp.concatenate([v[0, slot], v[1, slot]], axis=1))
        product = jnp.dot(wcat[b], jnp.concatenate(picks, axis=0), preferred_element_type=f32)
        return (product[:blk, :queries] + product[blk:, :queries]) + (product[:blk, queries:] + product[blk:, queries:])

    zero = jnp.zeros((8, queries), f32)

    own_copy.wait()

    @pl.loop(1, n)
    def _(i):
        q_arrival(lax.rem(me + i, n)).wait_recv()

    width = gathered.shape[2]
    flat = gathered[...].reshape(n * pad, width)
    row = lax.broadcasted_iota(jnp.int32, (queries, n * pad), 0)
    col = lax.broadcasted_iota(jnp.int32, (queries, n * pad), 1)
    for part in range(split):
        wanted = (row // own) * pad + part * own + row % own
        chosen = jnp.where(col == wanted, 1.0, 0.0).astype(bf16)
        query[:, part * width:(part + 1) * width] = jnp.dot(chosen, flat, preferred_element_type=f32).astype(bf16)

    per = nblk // chunks
    for i in range(chunks):
        db_copy(i).wait()

    @pl.loop(0, chunks, init_carry=zero)
    def norm0(i, carry):
        scores = lax.dot_general(
            db[pl.ds(i * chunk, chunk), :], query[...], (((1,), (1,)), ((), ())), preferred_element_type=f32
        )
        for t in range(per):
            b = i * per + t
            probed = jnp.max(jnp.where(probes_ref[...] == bl_ref[b, 0], 1.0, 0.0), axis=0, keepdims=True)
            seed = jnp.where(probed > 0.5, jnp.exp(scores[t * blk:(t + 1) * blk]), 0.0)
            base[b] = seed
            put(v0, half + b, root[b] * seed)
            carry = carry + fold(seed * seed)
        return carry

    halo_start(v0, 0)
    halo_wait(v0, 0)

    @pl.loop(0, nblk, init_carry=zero)
    def curve0(b, carry):
        seed = base[b]
        image = seed - damping * root[b] * weighed(v0, b)
        wide0[b] = image
        put(v1, half + b, root[b] * image)
        return carry + fold(seed * image)

    halo_start(v1, 1)
    reduce_start(red0, 0, norm0, curve0)
    gamma0, delta0 = reduce_wait(red0, 0)
    alpha0 = gamma0 / delta0
    halo_wait(v1, 1)

    @pl.loop(0, nblk, init_carry=(zero, zero))
    def dots1(b, carry):
        image = wide0[b]
        second = image - damping * root[b] * weighed(v1, b)
        residual = base[b] - alpha0 * image
        wide = image - alpha0 * second
        res1[b] = residual
        wide1[b] = wide
        put(v2, half + b, root[b] * wide)
        return carry[0] + fold(residual * residual), carry[1] + fold(residual * wide)

    halo_start(v2, 2, both=False)
    reduce_start(red1, 1, *dots1)
    gamma1, delta1 = reduce_wait(red1, 1)
    beta0 = gamma1 / gamma0
    alpha1 = gamma1 / (delta1 - beta0 * gamma1 / alpha0)

    @pl.loop(0, nblk, init_carry=zero)
    def norm2(b, carry):
        residual = res1[b] - alpha1 * (wide1[b] + beta0 * wide0[b])
        res2[b] = residual
        dir1[b] = res1[b] + beta0 * base[b]
        put(v3, half + b, root[b] * residual)
        return carry + fold(residual * residual)

    halo_wait(v2, 2, both=False)

    @pl.loop(half + nblk, 2 * nblk)
    def _(c):
        def value(v):
            return v[0, c].astype(f32) + v[1, c].astype(f32)
        first = value(v1)
        u = (value(v0) - alpha0 * first) - alpha1 * (value(v2) + beta0 * first)
        put(v3, c, 2.0 * u)

    @pl.loop(0, nblk, init_carry=zero)
    def cross2(b, carry):
        return carry + fold(res2[b] * root[b] * weighed(v3, b))

    reduce_start(red2, 2, norm2, norm2 - damping * cross2)
    gamma2, delta2 = reduce_wait(red2, 2)
    beta1 = gamma2 / gamma1
    alpha2 = gamma2 / (delta2 - beta1 * gamma2 / alpha1)
    gain = alpha1 + alpha2 * beta1

    @pl.loop(0, nblk)
    def _(b):
        out_ref[pl.ds(b * blk, blk), :] = alpha0 * base[b] + gain * dir1[b] + alpha2 * res2[b]

    halo_sent(v0, 0)
    halo_sent(v1, 1)
    halo_sent(v2, 2, both=False)

    @pl.loop(1, n)
    def _(i):
        peer = lax.rem(me + i, n)
        q_copy(peer).wait_send()
        red_copy(red0, 0, peer, me).wait_send()
        red_copy(red1, 1, peer, me).wait_send()
        red_copy(red2, 2, peer, me).wait_send()


def on_device(database, queries, probes, block_list, neighbors, affinity):
    nblk, cols, blk, _ = affinity.shape
    query_count = probes.shape[0]
    sub = lax.axis_size("sub")
    n = lax.axis_size("rows") * sub
    own, depth = queries.shape
    pad = 16
    split = max(1, pad // own) if own * 2 >= pad else 1
    pieces = queries.reshape(own, split, depth // split).transpose(1, 0, 2).reshape(own * split, depth // split)
    pad = -(-own * split // pad) * pad
    pieces = jnp.pad(pieces, ((0, pad - own * split), (0, 0)))
    vmem = pl.BlockSpec(memory_space=pltpu.VMEM)
    smem = pl.BlockSpec(memory_space=pltpu.SMEM)
    anywhere = pl.BlockSpec(memory_space=pl.ANY)
    blocks = pltpu.VMEM((nblk, blk, query_count), f32)
    zone = pltpu.VMEM((2, 2 * nblk, blk, query_count), bf16)
    sums = pltpu.VMEM((n, 16, query_count), f32)
    chunks = 4 if nblk % 4 == 0 else 1
    return pl.pallas_call(
        functools.partial(kernel, n, sub, pad, own, split),
        out_shape=jax.ShapeDtypeStruct((nblk * blk, query_count), f32),
        in_specs=[smem, smem, vmem, vmem, anywhere, anywhere],
        out_specs=vmem,
        scratch_shapes=[
            pltpu.VMEM((n, pad, depth // split), bf16),
            pltpu.VMEM((query_count, depth), bf16),
            pltpu.VMEM(database.shape, bf16),
            pltpu.VMEM(affinity.shape, f32),
            pltpu.VMEM((nblk, 2 * blk, cols * blk), bf16),
            blocks,
            zone, zone, zone, zone,
            blocks, blocks, blocks, blocks, blocks, blocks,
            sums, sums, sums,
            pltpu.SemaphoreType.DMA((nblk,)),
            pltpu.SemaphoreType.DMA((chunks,)),
            pltpu.SemaphoreType.DMA,
            pltpu.SemaphoreType.DMA((n,)),
            pltpu.SemaphoreType.DMA((n,)),
            pltpu.SemaphoreType.DMA((6,)),
            pltpu.SemaphoreType.DMA((6,)),
            pltpu.SemaphoreType.DMA((3, n)),
            pltpu.SemaphoreType.DMA((3, n)),
        ],
        compiler_params=pltpu.CompilerParams(
            collective_id=0, has_side_effects=True, vmem_limit_bytes=56 * 1024 * 1024
        ),
    )(neighbors, block_list, probes.T, pieces, database, affinity)


def solution(mesh):
    placed = (
        P(("groups", "rows", "sub"), None),
        P(("groups", "rows", "sub"), None),
        P("groups", None),
        P(("groups", "rows", "sub"), None),
        P(("groups", "rows", "sub"), None),
        P(("groups", "rows", "sub"), None, None, None),
    )
    return jax.shard_map(
        on_device,
        mesh=mesh,
        in_specs=placed,
        out_specs=P(("groups", "rows", "sub"), None),
        check_vma=False,
    )
```

time: 260 us -> 70 us (0.27)
  blocking collectives: 188 us -> 0 us
  Pallas kernels: 0 us -> 65 us
  matrix products: 33.1 us -> 0 us
  starting transfers between devices: 9.92 us -> 0 us
  other arithmetic: 9.14 us -> 0 us
  local copies, waits for them, and re-layouts: 12.1 us -> 4.75 us
  waiting for transfers between devices: 6.63 us -> 0 us
    psum x5 -> x0, blocking collectives: 164 us -> none  [the longest x3 93.9 us: squares(): return lax.psum(jnp.sum(residual * residual, axis=0), ('rows', 'sub'))]
    pallas_call x0 -> x1, Pallas kernels: none -> 65 us  [on_device(): pl.pallas_call(functools.partial(kernel, n, sub, pad, own, split), out_sh...]
    dot_general x4 -> x0, matrix products: 33.1 us -> none  [the longest x3 29.4 us: on_device(): jnp.einsum('ijrs,ijsq->irq', affinity, picked, precision=lax.Precision.HI...]
    all_gather x1 -> x0, blocking collectives: 24.2 us -> none  [on_device(): lax.all_gather(queries, ('rows', 'sub'), axis=0, tiled=True)]
    gather x3 -> x0, local copies, waits for them, and re-layouts: 10.8 us -> none  [on_device(): picked = stacked[local_slot]]
    ppermute x6 -> x0, starting transfers between devices: 9.92 us -> none  [the longest x3 5.87 us: with_halo(): before = lax.ppermute(last, axis, up)]
    ppermute x6 -> x0, waiting for transfers between devices: 6.63 us -> none  [the longest x3 6.62 us: with_halo(): after = lax.ppermute(initial, axis, down)]
    reduce_sum x6 -> x0, other arithmetic: 5.85 us -> none  [the longest x1 3.18 us: on_device(): degree = jnp.sum(affinity, axis=(1, 3)).reshape(-1, 1)]
  transfers between devices with their start and end apart: 6 -> 0, of which waited for: 3 -> 0; matrix products, arithmetic and copies ran while one was open for 0% -> 0% of each run, Pallas kernels for 0% -> 0%
where the time goes in v1:
time: 70 us; the launch traced here: 69.8 us
  Pallas kernels  65 us (93%)
  local copies, waits for them, and re-layouts  4.75 us (7%)
    pallas_call x1, Pallas kernels, on_device(): pl.pallas_call(functools.partial(kernel, n, sub, pad, own, split), out_sh...  65 us
    unnamed x3, local copies, waits for them, and re-layouts  4.75 us

profile of v1, /device:TPU:0, one launch (start us, length us, event | category | flops | bytes accessed | tf_op | source)
XLA Modules:
  0.0 69.8 jit_solution(8916903227570354635)
XLA Ops:
  0.0 1.3 %copy.8.bl_ref = s32[12,1]{1,0:T(8,128)} copy(s32[12,1]{0,1:T(1,128)} %param.9) | data formatting | bytes 96 | tf_op args[3]
  1.3 1.4 %copy.7.nb_ref = s32[12,8]{1,0:T(8,128)} copy(s32[12,8]{0,1:T(8,128)} %param.10) | data formatting | bytes 768 | tf_op args[4]
  2.7 65.0 %shard_map.64 = f32[1536,128]{1,0:T(8,128)} custom-call(s32[12,8]{1,0:T(8,128)} %copy.7.nb_ref, s32[12,1]{1,0:T(8,128)} %copy.8.bl_ref, s32[12,128]{1,0:T(8,128)} %bitcast.7, bf16[16,768]{1,0:T(8,128)(2,1)} %bitcast.6, bf16[1536,1536]{1,0:T(8,128)(2,1)} %db_hbm.1, f32[12,8,128,128]{3,2,1,0:T(8,128)} %aff_hbm.1), custom_call_target="tpu_custom_call" | custom-call | tf_op jit(solution)/shard_map/pallas_call | solution.py:304
  67.7 2.1 %copy.10 = f32[1536,128]{1,0:T(8,128)} copy(f32[1536,128]{1,0:T(8,128)} %shard_map.64) | data formatting | bytes 1572864

commit v2 on v1

v2 whole, which is shorter than its diff:
```python
import functools

import jax
import jax.numpy as jnp
from jax import lax
from jax.experimental import pallas as pl
from jax.experimental.pallas import tpu as pltpu
from jax.sharding import PartitionSpec as P

ITERS = 3
damping = 0.99
UNROLL = 3
PARTS = (2, 2, 1)
MESH = pl.DeviceIdType.MESH
f32, bf16 = jnp.float32, jnp.bfloat16


def kernel(
    n, sub, pad, own, split,
    nb_hbm, bl_hbm, probes_ref, q_ref, db_hbm, aff_hbm,
    out_ref,
    nb_ref, bl_ref, gathered, query, db, aff, wcat, root,
    v0, v1, v2, base, wide0, wide1, wide2, res2,
    red0, red1, red2,
    small_sem, aff_sem, db_sem, own_sem, q_send, q_recv, pass_send, pass_recv, halo_send, halo_recv, red_send, red_recv,
):
    nblk, cols, blk, _ = aff.shape
    half = nblk // 2
    queries = out_ref.shape[1]
    me = lax.axis_index("rows") * sub + lax.axis_index("sub")

    def place(index):
        return {"rows": index // sub, "sub": lax.rem(index, sub)}

    def aff_copy(b):
        return pltpu.make_async_copy(aff_hbm.at[b], aff.at[b], aff_sem.at[b])

    chunks = db_sem.shape[0]
    chunk = db.shape[0] // chunks

    def db_copy(i):
        rows = pl.ds(i * chunk, chunk)
        return pltpu.make_async_copy(db_hbm.at[rows], db.at[rows], db_sem.at[i])

    nb_copy = pltpu.make_async_copy(nb_hbm, nb_ref, small_sem.at[0])
    bl_copy = pltpu.make_async_copy(bl_hbm, bl_ref, small_sem.at[1])
    nb_copy.start()
    bl_copy.start()
    own_copy = pltpu.make_async_copy(q_ref, gathered.at[me], own_sem)
    own_copy.start()
    for b in range(nblk):
        aff_copy(b).start()
    for i in range(chunks):
        db_copy(i).start()

    for v in (v0, v1, v2):
        v[:, :half] = jnp.zeros((2, half, blk, queries), bf16)
        v[:, half + nblk:] = jnp.zeros((2, half, blk, queries), bf16)

    barrier = pltpu.get_barrier_semaphore()

    @pl.loop(1, n)
    def _(i):
        pl.semaphore_signal(barrier, inc=1, device_id=place(lax.rem(me + i, n)), device_id_type=MESH)

    pl.semaphore_wait(barrier, n - 1)

    my_row, my_sub = me // sub, lax.rem(me, sub)
    rows = n // sub

    def q_copy(peer, slot):
        return pltpu.make_async_remote_copy(
            src_ref=q_ref, dst_ref=gathered.at[slot], send_sem=q_send.at[peer], recv_sem=q_recv.at[slot],
            device_id=place(peer), device_id_type=MESH,
        )

    def q_pass(slot, there, other):
        return pltpu.make_async_remote_copy(
            src_ref=gathered.at[slot], dst_ref=gathered.at[there],
            send_sem=pass_send.at[slot, other], recv_sem=pass_recv.at[there],
            device_id=place(my_row * sub + other), device_id_type=MESH,
        )

    @pl.loop(1, rows)
    def _(i):
        q_copy(lax.rem(my_row + i, rows) * sub + my_sub, me).start()

    own_copy.wait()
    for k in range(1, sub):
        q_pass(me, me, lax.rem(my_sub + k, sub)).start()

    @pl.loop(0, nblk)
    def _(b):
        aff_copy(b).wait()
        total = jnp.zeros((blk, blk), f32)
        for j in range(cols):
            w = aff[b, j]
            total = total + w
            hi = w.astype(bf16)
            wcat[b, :blk, j * blk:(j + 1) * blk] = hi
            wcat[b, blk:, j * blk:(j + 1) * blk] = (w - hi.astype(f32)).astype(bf16)
        degree = jnp.sum(total, axis=1, keepdims=True)
        root[b] = jnp.broadcast_to(1.0 / jnp.sqrt(degree), (blk, queries))

    def put(v, index, u):
        hi = u.astype(bf16)
        v[0, index] = hi
        v[1, index] = (u - hi.astype(f32)).astype(bf16)

    def halo_copy(v, k, down, i):
        start, land = (half, half + nblk) if down else (nblk, 0)
        peer = jnp.maximum(me - 1, 0) if down else jnp.minimum(me + 1, n - 1)
        return pltpu.make_async_remote_copy(
            src_ref=v.at[pl.ds(0, PARTS[k]), start + i],
            dst_ref=v.at[pl.ds(0, PARTS[k]), land + i],
            send_sem=halo_send.at[2 * k + down, i], recv_sem=halo_recv.at[2 * k + down, i],
            device_id=place(peer), device_id_type=MESH,
        )

    def halo_start(v, k, i):
        @pl.when(me > 0)
        def _():
            halo_copy(v, k, 1, i).start()
        @pl.when(me < n - 1)
        def _():
            halo_copy(v, k, 0, i).start()

    def halo_wait(v, k):
        @pl.when(me < n - 1)
        def _():
            @pl.loop(0, half)
            def _(i):
                halo_copy(v, k, 1, i).wait_recv()
        @pl.when(me > 0)
        def _():
            @pl.loop(0, half)
            def _(i):
                halo_copy(v, k, 0, i).wait_recv()

    def halo_sent(v, k):
        @pl.when(me > 0)
        def _():
            @pl.loop(0, half)
            def _(i):
                halo_copy(v, k, 1, i).wait_send()
        @pl.when(me < n - 1)
        def _():
            @pl.loop(0, half)
            def _(i):
                halo_copy(v, k, 0, i).wait_send()

    def red_copy(red, k, peer, slot):
        return pltpu.make_async_remote_copy(
            src_ref=red.at[me], dst_ref=red.at[slot], send_sem=red_send.at[k, peer], recv_sem=red_recv.at[k, slot],
            device_id=place(peer), device_id_type=MESH,
        )

    def reduce_start(red, k, first, second):
        red[me] = jnp.concatenate(
            [jnp.sum(first, axis=0, keepdims=True), jnp.sum(second, axis=0, keepdims=True)], axis=0
        )

        @pl.loop(1, n)
        def _(i):
            peer = lax.rem(me + i, n)
            red_copy(red, k, peer, me).start()

    def reduce_wait(red, k):
        @pl.loop(1, n)
        def _(i):
            peer = lax.rem(me + i, n)
            red_copy(red, k, peer, peer).wait_recv()

        total = jnp.sum(red[...], axis=0)
        return total[:1], total[1:]

    def fold(values):
        return jnp.sum(values.reshape(blk // 8, 8, queries), axis=0)

    def weighed(v, b):
        picks = []
        for j in range(cols):
            slot = jnp.clip(nb_ref[b, j] - me * nblk + half, 0, 2 * nblk - 1)
            picks.append(jnp.concatenate([v[0, slot], v[1, slot]], axis=1))
        product = jnp.dot(wcat[b], jnp.concatenate(picks, axis=0), preferred_element_type=f32)
        return (product[:blk, :queries] + product[blk:, :queries]) + (product[:blk, queries:] + product[blk:, queries:])

    zero = jnp.zeros((8, queries), f32)

    @pl.loop(1, rows)
    def _(i):
        slot = lax.rem(my_row + i, rows) * sub + my_sub
        q_copy(slot, slot).wait_recv()
        for k in range(1, sub):
            q_pass(slot, slot, lax.rem(my_sub + k, sub)).start()

    @pl.loop(0, rows)
    def _(i):
        row = lax.rem(my_row + i, rows)
        for k in range(1, sub):
            other = lax.rem(my_sub + k, sub)
            q_pass(row * sub + my_sub, row * sub + other, other).wait_recv()

    width = gathered.shape[2]
    flat = gathered[...].reshape(n * pad, width)
    row = lax.broadcasted_iota(jnp.int32, (queries, n * pad), 0)
    col = lax.broadcasted_iota(jnp.int32, (queries, n * pad), 1)
    for part in range(split):
        wanted = (row // own) * pad + part * own + row % own
        chosen = jnp.where(col == wanted, 1.0, 0.0).astype(bf16)
        query[:, part * width:(part + 1) * width] = jnp.dot(chosen, flat, preferred_element_type=f32).astype(bf16)

    for i in range(chunks):
        db_copy(i).wait()
    nb_copy.wait()
    bl_copy.wait()
    per = half // (chunks // 2)

    @pl.loop(0, chunks // 2, init_carry=zero)
    def norm0(i, carry):
        for side in range(2):
            first = side * half + i * per
            scores = lax.dot_general(
                db[pl.ds(first * blk, per * blk), :], query[...], (((1,), (1,)), ((), ())),
                preferred_element_type=f32,
            )
            for t in range(per):
                b = first + t
                probed = jnp.max(jnp.where(probes_ref[...] == bl_ref[b, 0], 1.0, 0.0), axis=0, keepdims=True)
                seed = jnp.where(probed > 0.5, jnp.exp(scores[t * blk:(t + 1) * blk]), 0.0)
                base[b] = seed
                put(v0, half + b, root[b] * seed)
                carry = carry + fold(seed * seed)
        for t in range(per):
            halo_start(v0, 0, i * per + t)
        return carry

    halo_wait(v0, 0)

    @pl.loop(0, half, init_carry=zero, unroll=UNROLL)
    def curve0(i, carry):
        for b in (i, half + i):
            seed = base[b]
            image = seed - damping * root[b] * weighed(v0, b)
            wide0[b] = image
            put(v1, half + b, root[b] * image)
            carry = carry + fold(seed * image)
        halo_start(v1, 1, i)
        return carry

    reduce_start(red0, 0, norm0, curve0)
    halo_wait(v1, 1)

    @pl.loop(0, half, unroll=UNROLL)
    def _(i):
        for b in (i, half + i):
            image = wide0[b] - damping * root[b] * weighed(v1, b)
            wide1[b] = image
            put(v2, half + b, root[b] * image)
        halo_start(v2, 2, i)

    gamma0, delta0 = reduce_wait(red0, 0)
    alpha0 = gamma0 / delta0

    def first_residual(b):
        return base[b] - alpha0 * wide0[b], wide0[b] - alpha0 * wide1[b]

    @pl.loop(0, nblk, init_carry=(zero, zero))
    def dots1(b, carry):
        residual, image = first_residual(b)
        return carry[0] + fold(residual * residual), carry[1] + fold(residual * image)

    reduce_start(red1, 1, *dots1)
    halo_wait(v2, 2)

    @pl.loop(0, half, unroll=UNROLL)
    def _(i):
        for b in (i, half + i):
            wide2[b] = wide1[b] - damping * root[b] * weighed(v2, b)

    gamma1, delta1 = reduce_wait(red1, 1)
    beta0 = gamma1 / gamma0
    alpha1 = gamma1 / (delta1 - beta0 * gamma1 / alpha0)

    @pl.loop(0, nblk, init_carry=(zero, zero))
    def dots2(b, carry):
        residual, image = first_residual(b)
        second = wide1[b] - alpha0 * wide2[b]
        later = residual - alpha1 * (image + beta0 * wide0[b])
        image = image - alpha1 * (second + beta0 * wide1[b])
        res2[b] = later
        return carry[0] + fold(later * later), carry[1] + fold(later * image)

    reduce_start(red2, 2, *dots2)
    gamma2, delta2 = reduce_wait(red2, 2)
    beta1 = gamma2 / gamma1
    alpha2 = gamma2 / (delta2 - beta1 * gamma2 / alpha1)
    gain = alpha1 + alpha2 * beta1
    on_base = alpha0 + gain * (1.0 + beta0)
    on_wide = gain * alpha0

    @pl.loop(0, nblk)
    def _(b):
        out_ref[pl.ds(b * blk, blk), :] = on_base * base[b] - on_wide * wide0[b] + alpha2 * res2[b]

    halo_sent(v0, 0)
    halo_sent(v1, 1)
    halo_sent(v2, 2)

    @pl.loop(1, n)
    def _(i):
        peer = lax.rem(me + i, n)
        red_copy(red0, 0, peer, me).wait_send()
        red_copy(red1, 1, peer, me).wait_send()
        red_copy(red2, 2, peer, me).wait_send()

    @pl.loop(1, rows)
    def _(i):
        q_copy(lax.rem(my_row + i, rows) * sub + my_sub, me).wait_send()

    @pl.loop(0, rows)
    def _(i):
        slot = lax.rem(my_row + i, rows) * sub + my_sub
        for k in range(1, sub):
            q_pass(slot, slot, lax.rem(my_sub + k, sub)).wait_send()


def on_device(database, queries, probes, block_list, neighbors, affinity):
    nblk, cols, blk, _ = affinity.shape
    query_count = probes.shape[0]
    sub = lax.axis_size("sub")
    n = lax.axis_size("rows") * sub
    own, depth = queries.shape
    pad = 16
    split = max(1, pad // own) if own * 2 >= pad else 1
    pieces = queries.reshape(own, split, depth // split).transpose(1, 0, 2).reshape(own * split, depth // split)
    pad = -(-own * split // pad) * pad
    pieces = jnp.pad(pieces, ((0, pad - own * split), (0, 0)))
    vmem = pl.BlockSpec(memory_space=pltpu.VMEM)
    anywhere = pl.BlockSpec(memory_space=pl.ANY)
    blocks = pltpu.VMEM((nblk, blk, query_count), f32)
    zone = pltpu.VMEM((2, 2 * nblk, blk, query_count), bf16)
    sums = pltpu.VMEM((n, 2, query_count), f32)
    chunks = 6 if nblk % 12 == 0 else 2
    return pl.pallas_call(
        functools.partial(kernel, n, sub, pad, own, split),
        out_shape=jax.ShapeDtypeStruct((nblk * blk, query_count), f32),
        in_specs=[anywhere, anywhere, vmem, vmem, anywhere, anywhere],
        out_specs=vmem,
        scratch_shapes=[
            pltpu.SMEM(neighbors.shape, jnp.int32),
            pltpu.SMEM(block_list.shape, jnp.int32),
            pltpu.VMEM((n, pad, depth // split), bf16),
            pltpu.VMEM((query_count, depth), bf16),
            pltpu.VMEM(database.shape, bf16),
            pltpu.VMEM(affinity.shape, f32),
            pltpu.VMEM((nblk, 2 * blk, cols * blk), bf16),
            blocks,
            zone, zone, zone,
            blocks, blocks, blocks, blocks, blocks,
            sums, sums, sums,
            pltpu.SemaphoreType.DMA((2,)),
            pltpu.SemaphoreType.DMA((nblk,)),
            pltpu.SemaphoreType.DMA((chunks,)),
            pltpu.SemaphoreType.DMA,
            pltpu.SemaphoreType.DMA((n,)),
            pltpu.SemaphoreType.DMA((n,)),
            pltpu.SemaphoreType.DMA((n, sub)),
            pltpu.SemaphoreType.DMA((n,)),
            pltpu.SemaphoreType.DMA((6, nblk // 2)),
            pltpu.SemaphoreType.DMA((6, nblk // 2)),
            pltpu.SemaphoreType.DMA((3, n)),
            pltpu.SemaphoreType.DMA((3, n)),
        ],
        compiler_params=pltpu.CompilerParams(
            collective_id=0, has_side_effects=True, vmem_limit_bytes=56 * 1024 * 1024
        ),
    )(neighbors, block_list, probes.T, pieces, database, affinity)


def solution(mesh):
    placed = (
        P(("groups", "rows", "sub"), None),
        P(("groups", "rows", "sub"), None),
        P("groups", None),
        P(("groups", "rows", "sub"), None),
        P(("groups", "rows", "sub"), None),
        P(("groups", "rows", "sub"), None, None, None),
    )
    return jax.shard_map(
        on_device,
        mesh=mesh,
        in_specs=placed,
        out_specs=P(("groups", "rows", "sub"), None),
        check_vma=False,
    )
```

time: 70 us -> 58.8 us (0.84)
  Pallas kernels: 65 us -> 53.7 us
    pallas_call x1, Pallas kernels: 65 us -> 53.7 us  [on_device(): pl.pallas_call(functools.partial(kernel, n, sub, pad, own, split), out_sh...]
where the time goes in v2:
time: 58.8 us; the launch traced here: 58.5 us
  Pallas kernels  53.7 us (91%)
  local copies, waits for them, and re-layouts  4.75 us (8%)
    pallas_call x1, Pallas kernels, on_device(): pl.pallas_call(functools.partial(kernel, n, sub, pad, own, split), out_sh...  53.7 us
    unnamed x3, local copies, waits for them, and re-layouts  4.75 us

profile of v2, /device:TPU:0, one launch (start us, length us, event | category | flops | bytes accessed | tf_op | source)
XLA Modules:
  0.0 58.5 jit_solution(10418858864810694504)
XLA Ops:
  0.0 1.3 %copy.8.bl_hbm = s32[12,1]{1,0:T(8,128)} copy(s32[12,1]{0,1:T(1,128)} %param.9) | data formatting | bytes 96 | tf_op args[3]
  1.3 1.4 %copy.7.nb_hbm = s32[12,8]{1,0:T(8,128)} copy(s32[12,8]{0,1:T(8,128)} %param.10) | data formatting | bytes 768 | tf_op args[4]
  2.7 53.7 %shard_map.64 = f32[1536,128]{1,0:T(8,128)} custom-call(s32[12,8]{1,0:T(8,128)} %copy.7.nb_hbm, s32[12,1]{1,0:T(8,128)} %copy.8.bl_hbm, s32[12,128]{1,0:T(8,128)} %bitcast.7, bf16[16,768]{1,0:T(8,128)(2,1)} %bitcast.6, bf16[1536,1536]{1,0:T(8,128)(2,1)} %db_hbm.1, f32[12,8,128,128]{3,2,1,0:T(8,128)} %aff_hbm.1), custom_call_target="tpu_custom_call" | custom-call | tf_op jit(solution)/shard_map/pallas_call | solution.py:345
  56.4 2.1 %copy.10 = f32[1536,128]{1,0:T(8,128)} copy(f32[1536,128]{1,0:T(8,128)} %shard_map.64) | data formatting | bytes 1572864

commit v3 on v2

--- a/solution.py
+++ b/solution.py
@@ -10,7 +10,7 @@
 ITERS = 3
 damping = 0.99
 UNROLL = 3
-PARTS = (2, 2, 1)
+PARTS = (2, 1, 1)
 MESH = pl.DeviceIdType.MESH
 f32, bf16 = jnp.float32, jnp.bfloat16
 
@@ -20,7 +20,7 @@
     nb_hbm, bl_hbm, probes_ref, q_ref, db_hbm, aff_hbm,
     out_ref,
     nb_ref, bl_ref, gathered, query, db, aff, wcat, root,
-    v0, v1, v2, base, wide0, wide1, wide2, res2,
+    v0, v1, v2, t1, t2, base, wide0, wide1, wide2, res2,
     red0, red1, red2,
     small_sem, aff_sem, db_sem, own_sem, q_send, q_recv, pass_send, pass_recv, halo_send, halo_recv, red_send, red_recv,
 ):
@@ -53,9 +53,9 @@
     for i in range(chunks):
         db_copy(i).start()
 
-    for v in (v0, v1, v2):
-        v[:, :half] = jnp.zeros((2, half, blk, queries), bf16)
-        v[:, half + nblk:] = jnp.zeros((2, half, blk, queries), bf16)
+    for v in (v0, t1, t2):
+        v[:, :half] = jnp.zeros((v.shape[0], half, blk, queries), bf16)
+        v[:, half + nblk:] = jnp.zeros((v.shape[0], half, blk, queries), bf16)
 
     barrier = pltpu.get_barrier_semaphore()
 
@@ -184,6 +184,13 @@
             picks.append(jnp.concatenate([v[0, slot], v[1, slot]], axis=1))
         product = jnp.dot(wcat[b], jnp.concatenate(picks, axis=0), preferred_element_type=f32)
         return (product[:blk, :queries] + product[blk:, :queries]) + (product[:blk, queries:] + product[blk:, queries:])
+
+    def widen(v, before, change):
+        for start in (0, half + nblk):
+            @pl.loop(start, start + half)
+            def _(c):
+                known = before[0, c].astype(f32) + before[1, c].astype(f32)
+                put(v, c, known - change[0, c].astype(f32))
 
     zero = jnp.zeros((8, queries), f32)
 
@@ -241,23 +248,28 @@
     def curve0(i, carry):
         for b in (i, half + i):
             seed = base[b]
-            image = seed - damping * root[b] * weighed(v0, b)
+            drop = damping * root[b] * weighed(v0, b)
+            image = seed - drop
             wide0[b] = image
+            t1[0, half + b] = (root[b] * drop).astype(bf16)
             put(v1, half + b, root[b] * image)
             carry = carry + fold(seed * image)
-        halo_start(v1, 1, i)
+        halo_start(t1, 1, i)
         return carry
 
     reduce_start(red0, 0, norm0, curve0)
-    halo_wait(v1, 1)
+    halo_wait(t1, 1)
+    widen(v1, v0, t1)
 
     @pl.loop(0, half, unroll=UNROLL)
     def _(i):
         for b in (i, half + i):
-            image = wide0[b] - damping * root[b] * weighed(v1, b)
+            drop = damping * root[b] * weighed(v1, b)
+            image = wide0[b] - drop
             wide1[b] = image
+            t2[0, half + b] = (root[b] * drop).astype(bf16)
             put(v2, half + b, root[b] * image)
-        halo_start(v2, 2, i)
+        halo_start(t2, 2, i)
 
     gamma0, delta0 = reduce_wait(red0, 0)
     alpha0 = gamma0 / delta0
@@ -271,7 +283,8 @@
         return carry[0] + fold(residual * residual), carry[1] + fold(residual * image)
 
     reduce_start(red1, 1, *dots1)
-    halo_wait(v2, 2)
+    halo_wait(t2, 2)
+    widen(v2, v1, t2)
 
     @pl.loop(0, half, unroll=UNROLL)
     def _(i):
@@ -304,8 +317,8 @@
         out_ref[pl.ds(b * blk, blk), :] = on_base * base[b] - on_wide * wide0[b] + alpha2 * res2[b]
 
     halo_sent(v0, 0)
-    halo_sent(v1, 1)
-    halo_sent(v2, 2)
+    halo_sent(t1, 1)
+    halo_sent(t2, 2)
 
     @pl.loop(1, n)
     def _(i):
@@ -339,6 +352,7 @@
     vmem = pl.BlockSpec(memory_space=pltpu.VMEM)
     anywhere = pl.BlockSpec(memory_space=pl.ANY)
     blocks = pltpu.VMEM((nblk, blk, query_count), f32)
+    change = pltpu.VMEM((1, 2 * nblk, blk, query_count), bf16)
     zone = pltpu.VMEM((2, 2 * nblk, blk, query_count), bf16)
     sums = pltpu.VMEM((n, 2, query_count), f32)
     chunks = 6 if nblk % 12 == 0 else 2
@@ -356,7 +370,7 @@
             pltpu.VMEM(affinity.shape, f32),
             pltpu.VMEM((nblk, 2 * blk, cols * blk), bf16),
             blocks,
-            zone, zone, zone,
+            zone, zone, zone, change, change,
             blocks, blocks, blocks, blocks, blocks,
             sums, sums, sums,
             pltpu.SemaphoreType.DMA((2,)),

time: 58.8 us -> 53.3 us (0.906)
  Pallas kernels: 53.7 us -> 48.3 us
    pallas_call x1, Pallas kernels: 53.7 us -> 48.3 us  [on_device(): pl.pallas_call(functools.partial(kernel, n, sub, pad, own, split), out_sh...]
where the time goes in v3:
time: 53.3 us; the launch traced here: 53 us
  Pallas kernels  48.3 us (91%)
  local copies, waits for them, and re-layouts  4.75 us (9%)
    pallas_call x1, Pallas kernels, on_device(): pl.pallas_call(functools.partial(kernel, n, sub, pad, own, split), out_sh...  48.3 us
    unnamed x3, local copies, waits for them, and re-layouts  4.75 us

profile of v3, /device:TPU:0, one launch (start us, length us, event | category | flops | bytes accessed | tf_op | source)
XLA Modules:
  0.0 53.0 jit_solution(17808526912256062835)
XLA Ops:
  0.0 1.3 %copy.8.bl_hbm = s32[12,1]{1,0:T(8,128)} copy(s32[12,1]{0,1:T(1,128)} %param.9) | data formatting | bytes 96 | tf_op args[3]
  1.3 1.4 %copy.7.nb_hbm = s32[12,8]{1,0:T(8,128)} copy(s32[12,8]{0,1:T(8,128)} %param.10) | data formatting | bytes 768 | tf_op args[4]
  2.7 48.3 %shard_map.64 = f32[1536,128]{1,0:T(8,128)} custom-call(s32[12,8]{1,0:T(8,128)} %copy.7.nb_hbm, s32[12,1]{1,0:T(8,128)} %copy.8.bl_hbm, s32[12,128]{1,0:T(8,128)} %bitcast.7, bf16[16,768]{1,0:T(8,128)(2,1)} %bitcast.6, bf16[1536,1536]{1,0:T(8,128)(2,1)} %db_hbm.1, f32[12,8,128,128]{3,2,1,0:T(8,128)} %aff_hbm.1), custom_call_target="tpu_custom_call" | custom-call | tf_op jit(solution)/shard_map/pallas_call | solution.py:359
  51.0 2.1 %copy.10 = f32[1536,128]{1,0:T(8,128)} copy(f32[1536,128]{1,0:T(8,128)} %shard_map.64) | data formatting | bytes 1572864
